TPU v7x, 128 devices: a whole 4x4x4 slice. The times are simulated.
128 devices in a mesh: az: 16 (over y, x_lo, core), rad: 8 (over x_hi, z).
Axes of the slice: x: 4 (x_hi: 2, x_lo: 2; x = x_hi * 2 + x_lo), y: 4, z: 4, core: 2. Of those that a mesh axis runs over, the one named last changes fastest.
Arguments:
- density: float32 [128, 64, 4096], P('rad', None, 'az'), may hold values from 0.5 to 2
- momenta: float32 [3, 128, 64, 4096], P(None, 'rad', None, 'az'), may hold values from -0.75 to 0.75
- energy: float32 [128, 64, 4096], P('rad', None, 'az'), may hold values from 0.5 to 2
- shifts: int32 [128], P('rad'), may hold values from 0 to 4095, as said below
Outputs:
- density_next: float32 [128, 64, 4096], P('rad', None, 'az')
- momenta_next: float32 [3, 128, 64, 4096], P(None, 'rad', None, 'az')
- energy_next: float32 [128, 64, 4096], P('rad', None, 'az')
Inputs may be any that keep to these rules, and one draw needn't show every extreme that they name: `shifts`: any shift of 0 to 4095 may occur; both ends occur.
All inputs are finite; a program needn't handle non-finite values.
Results may differ from a plain program's by a relative error of at most 0.0003.
Values sent between devices are 32-bit elements; how exact they have to be, the bound alone decides.
A program may use at most 192 MiB of HBM per device.

v0:
```python
import jax
import jax.numpy as jnp
from jax import lax
from jax.sharding import PartitionSpec as P


def padded_2(x, sides, width, wrap):
    for axis, dim in sides:
        size, length = (lax.axis_size(axis), x.shape[dim])
        up = [(i, (i + 1) % size) for i in range(size if wrap else size - 1)]
        down = [(j, i) for i, j in up]
        last = lax.slice_in_dim(x, length - width, length, axis=dim)
        leading = lax.slice_in_dim(x, 0, width, axis=dim)
        before = lax.ppermute(last, axis, up)
        after = lax.ppermute(leading, axis, down)
        x = jnp.concatenate([before, x, after], axis=dim)
    return x


def from_behind(value, axis, steps):
    count = lax.axis_size(axis)
    pairs = [(source, (source + steps) % count) for source in range(count)]
    return lax.ppermute(value, axis, pairs)


def advance(padded, at_inner, at_outer, radius):
    rows = padded.shape[1] - 2
    rho = padded[0]
    vel_r = padded[1] / rho
    core = padded[:, :, :, 1:-1]
    face_r = 0.5 * (vel_r[:-1] + vel_r[1:])[:, :, 1:-1]
    flux_r = face_r * jnp.where(face_r > 0, core[:, :-1], core[:, 1:])
    faces = jnp.arange(rows + 1)
    keep = jnp.where((faces == 0) & at_inner, 0.0, 1.0)
    keep = jnp.where((faces == rows) & at_outer, 0.0, keep).astype(jnp.float32)
    flux_r = flux_r * keep[None, :, None, None]
    face_rad = 0.5 * (radius[:-1] + radius[1:])
    centre = radius[1:-1]
    weighted = flux_r * (face_rad * face_rad)[None, :, None, None]
    div_r = (weighted[:, 1:] - weighted[:, :-1]) / (centre * centre)[None, :, None, None]
    inner = padded[:, 1:-1]
    rho_in = inner[0]
    vel_p = inner[2] / rho_in
    vel_t = inner[3] / rho_in
    qcore = inner[..., 1:-1]
    vt_core = vel_t[..., 1:-1]
    face_t = 0.5 * (vt_core[:, :-1] + vt_core[:, 1:])
    flux_t = face_t * jnp.where(face_t > 0, qcore[:, :, :-1], qcore[:, :, 1:])
    zero_t = jnp.zeros_like(flux_t[:, :, :1])
    flux_t = jnp.concatenate([zero_t, flux_t, zero_t], axis=2)
    div_t = flux_t[:, :, 1:] - flux_t[:, :, :-1]
    face_p = 0.5 * (vel_p[..., :-1] + vel_p[..., 1:])
    flux_p = face_p * jnp.where(face_p > 0, inner[..., :-1], inner[..., 1:])
    div_p = flux_p[..., 1:] - flux_p[..., :-1]
    moved = qcore - div_r - div_t - div_p
    pressure = 0.4 * padded[4]
    grad_r = 0.5 * (pressure[2:, :, 1:-1] - pressure[:-2, :, 1:-1])
    grad_p = 0.5 * (pressure[1:-1, :, 2:] - pressure[1:-1, :, :-2])
    middle = pressure[1:-1, :, 1:-1]
    edged = jnp.concatenate([middle[:, :1], middle, middle[:, -1:]], axis=1)
    grad_t = 0.5 * (edged[:, 2:] - edged[:, :-2])
    pushed = moved[1:4] - 0.5 * jnp.stack([grad_r, grad_p, grad_t])
    return jnp.concatenate([moved[:1], pushed, moved[4:]], axis=0)


def per_device(density, momenta, energy, shifts):
    state = jnp.concatenate([density[None], momenta, energy[None]], axis=0)
    rows = state.shape[1]
    width = state.shape[3]
    position = lax.axis_index("rad")
    groups = lax.axis_size("rad")
    padded = padded_2(state, (("rad", 1),), 1, False)
    padded = padded_2(padded, (("az", 3),), 1, True)
    at_inner = position == 0
    at_outer = position == groups - 1
    lower = jnp.where(at_inner, padded[:, 1:2], padded[:, 0:1])
    upper = jnp.where(at_outer, padded[:, -2:-1], padded[:, -1:])
    padded = jnp.concatenate([lower, padded[:, 1:-1], upper], axis=1)
    index = (position * rows + jnp.arange(-1, rows + 1)).astype(jnp.float32)
    radius = 1.0 + 2.0 * (index + 0.5) / (groups * rows)
    moving = advance(padded, at_inner, at_outer, radius)
    owners = shifts // width
    rest = shifts % width
    levels = lax.axis_size("az").bit_length() - 1
    for level in range(levels):
        taken = owners >> level & 1 == 1
        moved_on = from_behind(moving, "az", 1 << level)
        moving = jnp.where(taken[None, :, None, None], moved_on, moving)
    previous = from_behind(moving, "az", 1)
    joined = jnp.concatenate([previous, moving], axis=3)

    def window(row, start):
        return lax.dynamic_slice_in_dim(row, start, width, axis=2)

    out = jax.vmap(window, in_axes=(1, 0), out_axes=1)(joined, width - rest)
    return (out[0], out[1:4], out[4])


def solution(mesh):
    return jax.shard_map(
        per_device,
        mesh=mesh,
        in_specs=(P("rad", None, "az"), P(None, "rad", None, "az"), P("rad", None, "az"), P("rad")),
        out_specs=(P("rad", None, "az"), P(None, "rad", None, "az"), P("rad", None, "az")),
        check_vma=False,
    )
```

profile of v0, /device:TPU:65, one launch (start us, length us, event | category | flops | bytes accessed | tf_op | source)
XLA Modules:
  0.0 678.5 jit_solution(15586684248077781454)
XLA Ops:
  0.6 3.3 pad_maximum_fusion.15
  7.2 3.2 collective-permute-start
  12.6 5.4 collective-permute-done
  22.9 3.6 fusion.31
  42.9 10.5 %pad_maximum_fusion.1 = f32[5,18,64,258]{3,2,1,0:T(8,128)} fusion(f32[5,18,64,1]{3,2,1,0:T(8,128)} %copy.24, f32[5,1,64,256]{3,2,1,0:T(8,128)} %collective-permute-done.1, f32[1,16,64,256]{3,2,1,0:T(8,128)} %bitcast.28, f32[3,16,64,256]{3,2,1,0:T(8,128)S(1)} %copy-done, f32[1,16,64,256]{3,2,1,0:T(8,128)} %bitcast.37, ...), kind=kLoop, calls=%fused_computation.2 | loop fusion | flops 8916480 | bytes 11888640 | tf_op jit(solution)/shard_map/concatenate | solution.py:16
  53.4 3.9 slice.241
  73.9 8.6 %fusion.7 = f32[5,16,63,256]{3,2,1,0:T(8,128)} fusion(f32[5,16,64,256]{3,2,1,0:T(8,128)} %copy-done.5, f32[16,63,256]{2,1,0:T(8,128)} %get-tuple-element.15, pred[16,63,256]{2,1,0:T(8,128)(4,1)} %get-tuple-element.14), kind=kLoop, calls=%fused_computation.25 | loop fusion | flops 2580480 | bytes 16773120 | tf_op jit(solution)/shard_map/mul | solution.py:48
  82.5 6.9 %fusion.5 = f32[5,17,64,256]{3,2,1,0:T(8,128)} fusion(f32[5,1,64,258]{3,2,1,0:T(8,128)} %copy-done.9, f32[5,16,64,258]{3,2,1,0:T(8,128)S(1)} %slice.241, f32[5,1,64,258]{3,2,1,0:T(8,128)} %copy-done.10, f32[17]{0:T(128)S(1)} %get-tuple-element.37, f32[17]{0:T(128)S(1)} %get-tuple-element.36, f32[17,64,256]{2,1,0:T(8,128)S(1)} %slice_multiply_fusion, ...), kind=kLoop, calls=%fused_computation.20 | loop fusion | flops 8355840 | bytes 12907656 | tf_op jit(solution)/shard_map/mul | solution.py:39
  89.4 6.2 fusion.1
  95.6 15.4 %fusion.6 = f32[5,16,64,256]{3,2,1,0:T(8,128)} fusion(f32[5,16,64,257]{3,2,1,0:T(8,128)} %fusion.1, f32[5,17,64,256]{3,2,1,0:T(8,128)} %fusion.5, f32[5,16,63,256]{3,2,1,0:T(8,128)} %fusion.7, f32[16]{0:T(128)S(1)} %slice_multiply_fusion.1, f32[1,16,64,256]{3,2,1,0:T(8,128)S(1)} %bitcast.34, f32[3,16,64,256]{3,2,1,0:T(8,128)S(1)} %copy-done, ...), kind=kLoop, calls=%fused_computation.23 | loop fusion | flops 11796480 | bytes 36618304 | tf_op jit(solution)/shard_map/sub | solution.py:55
  117.8 56.7 %collective-permute-done.4 = f32[5,16,64,256]{3,2,1,0:T(8,128)S(1)} collective-permute-done((f32[5,16,64,256]{3,2,1,0:T(8,128)S(1)}, f32[5,16,64,256]{3,2,1,0:T(8,128)S(1)}, u32[]{:S(2)}, u32[]{:S(2)}) %collective-permute-start.4) | collective-permute-done | bytes 5242912 | tf_op jit(solution)/shard_map/ppermute | solution.py:23
  178.2 112.6 %collective-permute-done.5 = f32[5,16,64,256]{3,2,1,0:T(8,128)S(1)} collective-permute-done((f32[5,16,64,256]{3,2,1,0:T(8,128)S(1)}, f32[5,16,64,256]{3,2,1,0:T(8,128)S(1)}, u32[]{:S(2)}, u32[]{:S(2)}) %collective-permute-start.5) | collective-permute-done | bytes 5242912 | tf_op jit(solution)/shard_map/ppermute | solution.py:23
  292.4 112.8 %collective-permute-done.6 = f32[5,16,64,256]{3,2,1,0:T(8,128)S(1)} collective-permute-done((f32[5,16,64,256]{3,2,1,0:T(8,128)S(1)}, f32[5,16,64,256]{3,2,1,0:T(8,128)S(1)}, u32[]{:S(2)}, u32[]{:S(2)}) %collective-permute-start.6) | collective-permute-done | bytes 5242912 | tf_op jit(solution)/shard_map/ppermute | solution.py:23
  406.8 4.9 collective-permute-start.7
  411.6 111.4 %collective-permute-done.7 = f32[5,16,64,256]{3,2,1,0:T(8,128)S(1)} collective-permute-done((f32[5,16,64,256]{3,2,1,0:T(8,128)S(1)}, f32[5,16,64,256]{3,2,1,0:T(8,128)S(1)}, u32[]{:S(2)}, u32[]{:S(2)}) %collective-permute-start.7) | collective-permute-done | bytes 5242912 | tf_op jit(solution)/shard_map/ppermute | solution.py:23
  527.0 7.1 %collective-permute-start.8 = (f32[5,16,64,256]{3,2,1,0:T(8,128)S(1)}, f32[5,16,64,256]{3,2,1,0:T(8,128)}, u32[]{:S(2)}, u32[]{:S(2)}) collective-permute-start(f32[5,16,64,256]{3,2,1,0:T(8,128)S(1)} %broadcast_select_fusion.3), channel_id=1, source_target_pairs={{0,8},{8,16},{16,24},{24,32},{32,40},{40,48},{48,56},{56,64},{64,7... | collective-permute-start | bytes 15728648 | tf_op jit(solution)/shard_map/ppermute | solution.py:23
  534.1 56.7 %collective-permute-done.8 = f32[5,16,64,256]{3,2,1,0:T(8,128)} collective-permute-done((f32[5,16,64,256]{3,2,1,0:T(8,128)S(1)}, f32[5,16,64,256]{3,2,1,0:T(8,128)}, u32[]{:S(2)}, u32[]{:S(2)}) %collective-permute-start.8) | collective-permute-done | bytes 5242912 | tf_op jit(solution)/shard_map/ppermute | solution.py:23
  590.8 9.9 %pad_maximum_fusion = f32[5,16,64,512]{3,2,1,0:T(8,128)} fusion(f32[5,16,64,256]{3,2,1,0:T(8,128)} %copy-done.6, f32[5,16,64,256]{3,2,1,0:T(8,128)} %collective-permute-done.8), kind=kLoop, calls=%fused_computation.1 | loop fusion | flops 2621440 | bytes 20971520 | tf_op jit(solution)/shard_map/concatenate | solution.py:90
  600.6 27.4 %copy.27 = f32[5,16,64,512]{2,0,1,3:T(8,128)} copy(f32[5,16,64,512]{3,2,1,0:T(8,128)} %pad_maximum_fusion) | data formatting | bytes 20971520 | tf_op jit(solution)/shard_map/concatenate | solution.py:90
  628.0 13.1 %gather_fusion = f32[16,5,64,256]{2,1,3,0:T(8,128)} fusion(f32[16,5,64,512]{2,1,0,3:T(8,128)} %bitcast.44, s32[16]{0:T(128)S(1)} %fusion.27), kind=kCustom, calls=%fused_computation | custom fusion | bytes 10486016 | tf_op jit(solution)/shard_map/vmap()/gather | solution.py:93
  641.2 15.0 %fusion.30 = (f32[1,16,64,256]{2,0,3,1:T(1,128)}, f32[1,16,64,256]{2,0,3,1:T(1,128)S(1)}) fusion(f32[5,16,64,256]{2,0,3,1:T(8,128)} %bitcast.45), kind=kLoop, calls=%fused_computation.89 | loop fusion | bytes 4194304 | tf_op jit(solution)/shard_map/slice | solution.py:96
  656.2 9.6 %slice.266 = f32[3,16,64,256]{2,0,3,1:T(4,128)} slice(f32[5,16,64,256]{2,0,3,1:T(8,128)} %bitcast.46), slice={[1:4], [0:16], [0:64], [0:256]} | slice | bytes 6291456 | tf_op jit(solution)/shard_map/slice | solution.py:96
  665.8 8.0 %copy.29 = f32[3,16,64,256]{3,2,1,0:T(8,128)} copy(f32[3,16,64,256]{2,0,3,1:T(4,128)} %slice.266) | data formatting | bytes 6291456
  673.8 3.1 copy.30
  (74 shorter events, 62.1 us)
Async XLA Ops:
  0.6 20.3 %copy-start = (f32[3,16,64,256]{3,2,1,0:T(8,128)S(1)}, f32[3,16,64,256]{3,2,1,0:T(8,128)}, u32[]{:S(2)}) copy-start(f32[3,16,64,256]{3,2,1,0:T(8,128)} %param.5) | copy-start | bytes 9437188
  3.9 2.4 copy-start.5
  7.2 10.8 %collective-permute-start = (f32[5,1,64,256]{3,2,1,0:T(8,128)}, f32[5,1,64,256]{3,2,1,0:T(8,128)S(1)}, u32[]{:S(2)}, u32[]{:S(2)}) collective-permute-start(f32[5,1,64,256]{3,2,1,0:T(8,128)} %get-tuple-element.26), channel_id=1, source_target_pairs={{0,1},{1,2},{2,3},{3,4},{4,5},{5,6},{6,7},{8,9},{9,10},{10,11},{11... | collective-permute-start | bytes 983048 | tf_op jit(solution)/shard_map/ppermute | solution.py:14
  10.5 10.5 %collective-permute-start.1 = (f32[5,1,64,256]{3,2,1,0:T(8,128)}, f32[5,1,64,256]{3,2,1,0:T(8,128)}, u32[]{:S(2)}, u32[]{:S(2)}) collective-permute-start(f32[5,1,64,256]{3,2,1,0:T(8,128)} %get-tuple-element.27), channel_id=1, source_target_pairs={{1,0},{2,1},{3,2},{4,3},{5,4},{6,5},{7,6},{9,8},{10,9},{11,10},{12... | collective-permute-start | bytes 983048 | tf_op jit(solution)/shard_map/ppermute | solution.py:15
  31.9 8.1 %collective-permute-start.3 = (f32[5,18,64,1]{2,3,1,0:T(1,128)S(1)}, f32[5,18,64,1]{2,3,1,0:T(1,128)}, u32[]{:S(2)}, u32[]{:S(2)}) collective-permute-start(f32[5,18,64,1]{2,3,1,0:T(1,128)S(1)} %copy.32), channel_id=1, source_target_pairs={{8,0},{16,8},{24,16},{32,24},{40,32},{48,40},{56,48},{64,56},{72,6... | collective-permute-start | bytes 69128 | tf_op jit(solution)/shard_map/ppermute | solution.py:15
  33.8 3.3 collective-permute-start.2
  53.4 4.1 copy-start.1
  53.4 5.0 copy-start.2
  53.4 5.2 copy-start.3
  53.4 5.5 copy-start.4
  61.0 0.8 copy-start.10
  82.5 6.9 %copy-start.8 = (f32[16,64,257]{2,1,0:T(8,128)S(1)}, f32[16,64,257]{2,1,0:T(8,128)}, u32[]{:S(2)}) copy-start(f32[16,64,257]{2,1,0:T(8,128)} %get-tuple-element.17) | copy-start | bytes 3158020
  82.5 6.9 %copy-start.14 = (pred[16,64,257]{2,1,0:T(8,128)(4,1)S(1)}, pred[16,64,257]{2,1,0:T(8,128)(4,1)}, u32[]{:S(2)}) copy-start(pred[16,64,257]{2,1,0:T(8,128)(4,1)} %get-tuple-element.16) | copy-start | bytes 789508
  95.6 17.3 %copy-start.13 = (f32[16,64,256]{2,1,0:T(8,128)S(1)}, f32[16,64,256]{2,1,0:T(8,128)}, u32[]{:S(2)}) copy-start(f32[16,64,256]{2,1,0:T(8,128)} %get-tuple-element.29) | copy-start | bytes 3145732
  95.6 17.6 %copy-start.12 = (f32[1,16,64,256]{3,2,1,0:T(8,128)S(1)}, f32[1,16,64,256]{3,2,1,0:T(8,128)}, u32[]{:S(2)}) copy-start(f32[1,16,64,256]{3,2,1,0:T(8,128)} %get-tuple-element.30) | copy-start | bytes 3145732
  111.1 3.1 copy-start.7
  111.1 3.4 copy-start.11
  115.1 2.6 copy-start.15
  115.7 58.7 %collective-permute-start.4 = (f32[5,16,64,256]{3,2,1,0:T(8,128)S(1)}, f32[5,16,64,256]{3,2,1,0:T(8,128)S(1)}, u32[]{:S(2)}, u32[]{:S(2)}) collective-permute-start(f32[5,16,64,256]{3,2,1,0:T(8,128)S(1)} %pad_maximum_fusion.16), channel_id=1, source_target_pairs={{0,8},{8,16},{16,24},{24,32},{32,40},{40,48},{48,56},{56,64},{64,7... | collective-permute-start | bytes 15728648 | tf_op jit(solution)/shard_map/ppermute | solution.py:23
  176.0 114.8 %collective-permute-start.5 = (f32[5,16,64,256]{3,2,1,0:T(8,128)S(1)}, f32[5,16,64,256]{3,2,1,0:T(8,128)S(1)}, u32[]{:S(2)}, u32[]{:S(2)}) collective-permute-start(f32[5,16,64,256]{3,2,1,0:T(8,128)S(1)} %broadcast_select_fusion), channel_id=1, source_target_pairs={{0,16},{8,24},{16,32},{24,40},{32,48},{40,56},{48,64},{56,72},{64,... | collective-permute-start | bytes 15728648 | tf_op jit(solution)/shard_map/ppermute | solution.py:23
  292.0 113.2 %collective-permute-start.6 = (f32[5,16,64,256]{3,2,1,0:T(8,128)S(1)}, f32[5,16,64,256]{3,2,1,0:T(8,128)S(1)}, u32[]{:S(2)}, u32[]{:S(2)}) collective-permute-start(f32[5,16,64,256]{3,2,1,0:T(8,128)S(1)} %broadcast_select_fusion.1), channel_id=1, source_target_pairs={{0,32},{8,40},{16,48},{24,56},{32,64},{40,72},{48,80},{56,88},{64,... | collective-permute-start | bytes 15728648 | tf_op jit(solution)/shard_map/ppermute | solution.py:23
  406.8 116.3 %collective-permute-start.7 = (f32[5,16,64,256]{3,2,1,0:T(8,128)S(1)}, f32[5,16,64,256]{3,2,1,0:T(8,128)S(1)}, u32[]{:S(2)}, u32[]{:S(2)}) collective-permute-start(f32[5,16,64,256]{3,2,1,0:T(8,128)S(1)} %broadcast_select_fusion.2), channel_id=1, source_target_pairs={{0,64},{8,72},{16,80},{24,88},{32,96},{40,104},{48,112},{56,120},{... | collective-permute-start | bytes 15728648 | tf_op jit(solution)/shard_map/ppermute | solution.py:23
  524.6 2.3 copy-start.6
  527.0 63.8 %collective-permute-start.8 = (f32[5,16,64,256]{3,2,1,0:T(8,128)S(1)}, f32[5,16,64,256]{3,2,1,0:T(8,128)}, u32[]{:S(2)}, u32[]{:S(2)}) collective-permute-start(f32[5,16,64,256]{3,2,1,0:T(8,128)S(1)} %broadcast_select_fusion.3), channel_id=1, source_target_pairs={{0,8},{8,16},{16,24},{24,32},{32,40},{40,48},{48,56},{56,64},{64,7... | collective-permute-start | bytes 15728648 | tf_op jit(solution)/shard_map/ppermute | solution.py:23
  (1 other events, 0.8 us)
where the time goes:
time: 683 us; the launch traced here: 678 us
  waiting for transfers between devices  460 us (67%)
  local copies, waits for them, and re-layouts  108 us (16%)
  other arithmetic  84.4 us (12%)
  starting transfers between devices  25.1 us (4%)
    ppermute x5, waiting for transfers between devices, from_behind(): return lax.ppermute(value, axis, pairs)  450 us
    concatenate x1, local copies, waits for them, and re-layouts, per_device(): joined = jnp.concatenate([previous, moving], axis=3)  27.4 us
    unnamed x37, local copies, waits for them, and re-layouts  26.3 us
    slice x2, local copies, waits for them, and re-layouts, per_device(): return (out[0], out[1:4], out[4])  24.6 us
    ppermute x5, starting transfers between devices, from_behind(): return lax.ppermute(value, axis, pairs)  16.6 us
    sub x1, other arithmetic, advance(): moved = qcore - div_r - div_t - div_p  15.4 us
  transfers between devices with their start and end apart: 9, of which 8 were waited for; matrix products, arithmetic and copies ran while one was open for 0% of the time, Pallas kernels for 0%

commit v1 on v0

v1 whole, which is shorter than its diff:
```python
import functools

import jax
import jax.numpy as jnp
from jax import lax
from jax.experimental import pallas as pl
from jax.experimental.pallas import tpu as pltpu
from jax.sharding import PartitionSpec as P

MESH = pl.DeviceIdType.MESH
LANES = 128
SUB = 8
FIELDS = 5


def remote(src, dst, send, recv, **where):
    return pltpu.make_async_remote_copy(
        src_ref=src, dst_ref=dst, send_sem=send, recv_sem=recv, device_id=where, device_id_type=MESH
    )


def wait_bytes(ref, sem):
    pltpu.make_async_copy(ref, ref, sem).wait()


def peer(me, k):
    y = (me // 4 + k // 4) % 4
    x = (me // 2 + k // 2) % 2
    core = (me + k) % 2
    return y * 4 + x * 2 + core


def kernel(chunks, early, den, mom, en, shifts, landed, *refs):
    amounts, st, send, turned, pack, halo = refs[:6]
    whole = refs[6 : 6 + chunks]
    in_sem, rad_send, rad_recv, az_send, az_recv, s1, r1, own1, s2, r2, own2 = refs[6 + chunks :]
    rows = den.shape[0]
    tiles = den.shape[1] // SUB
    per = tiles // chunks
    me = lax.axis_index("az")
    n = lax.axis_size("az")
    pos = lax.axis_index("rad")
    groups = lax.axis_size("rad")
    at_inner = pos == 0
    at_outer = pos == groups - 1

    loads = [
        pltpu.make_async_copy(den, st.at[0, pl.ds(1, rows)], in_sem.at[0]),
        pltpu.make_async_copy(mom, st.at[pl.ds(1, 3), pl.ds(1, rows)], in_sem.at[1]),
        pltpu.make_async_copy(en, st.at[4, pl.ds(1, rows)], in_sem.at[2]),
        pltpu.make_async_copy(shifts, amounts, in_sem.at[3]),
    ]
    for c in loads:
        c.start()

    barrier = pltpu.get_barrier_semaphore()

    def greet(k, _):
        pl.semaphore_signal(barrier, 1, device_id={"az": peer(me, k)}, device_id_type=MESH)
        return 0

    lax.fori_loop(1, n, greet, 0)

    @pl.when(jnp.logical_not(at_outer))
    def _():
        pl.semaphore_signal(barrier, 1, device_id={"rad": pos + 1}, device_id_type=MESH)

    @pl.when(jnp.logical_not(at_inner))
    def _():
        pl.semaphore_signal(barrier, 1, device_id={"rad": pos - 1}, device_id_type=MESH)

    apart = jnp.where(at_inner, 0, 1) + jnp.where(at_outer, 0, 1)
    pl.semaphore_wait(barrier, n - 1 + apart)

    def radial(row, slot, way, to):
        return [
            remote(den.at[row], st.at[0, slot], rad_send.at[way, 0], rad_recv.at[way, 0], rad=to),
            remote(mom.at[:, row], st.at[pl.ds(1, 3), slot], rad_send.at[way, 1], rad_recv.at[way, 1], rad=to),
            remote(en.at[row], st.at[4, slot], rad_send.at[way, 2], rad_recv.at[way, 2], rad=to),
        ]

    outward = radial(rows - 1, 0, 0, (pos + 1) % groups)
    inward = radial(0, rows + 1, 1, (pos + groups - 1) % groups)

    @pl.when(jnp.logical_not(at_outer))
    def _():
        for c in outward:
            c.start()

    @pl.when(jnp.logical_not(at_inner))
    def _():
        for c in inward:
            c.start()

    for c in loads:
        c.wait()

    lane = lax.broadcasted_iota(jnp.int32, (SUB, LANES), 1)
    sub = lax.broadcasted_iota(jnp.int32, (SUB, LANES), 0)

    def packing(t, _):
        at = pl.ds(pl.multiple_of(t * SUB, SUB), SUB)
        first = jnp.zeros((SUB, LANES), jnp.float32)
        last = jnp.zeros((SUB, LANES), jnp.float32)
        for f in range(FIELDS):
            for i in range(rows):
                k = f * rows + i
                low = st[f, 1 + i, at, 0:LANES]
                high = st[f, 1 + i, at, LANES : 2 * LANES]
                first = jnp.where(lane == k, pltpu.roll(low, k, 1) if k else low, first)
                last = jnp.where(lane == k, pltpu.roll(high, k + 1, 1), last)
        pack[0, t] = first
        pack[1, t] = last
        return 0

    lax.fori_loop(0, tiles, packing, 0)
    right = remote(pack.at[1], halo.at[0], az_send.at[0], az_recv.at[0], az=(me + 1) % n)
    left = remote(pack.at[0], halo.at[1], az_send.at[1], az_recv.at[1], az=(me + n - 1) % n)
    right.start()
    left.start()

    total = (groups * rows)

    def radius(index):
        return 1.0 + 2.0 * (index.astype(jnp.float32) + 0.5) / total

    def upwind(face, low, high):
        return face * jnp.where(face > 0, low, high)

    def compute(row, t):
        t0 = pl.multiple_of(t * SUB, SUB)
        at = pl.ds(t0, SUB)
        at_dn = pl.ds(pl.multiple_of(jnp.maximum(t - 1, 0) * SUB, SUB), SUB)
        at_up = pl.ds(pl.multiple_of(jnp.minimum(t + 1, tiles - 1) * SUB, SUB), SUB)
        index = pos * rows + row
        here = radius(index)
        face_up = 0.5 * (here + radius(index + 1))
        face_dn = 0.5 * (radius(index - 1) + here)
        area = jnp.full((SUB, LANES), here * here, jnp.float32)
        w_up = jnp.full((SUB, LANES), face_up * face_up, jnp.float32) / area
        w_dn = jnp.full((SUB, LANES), face_dn * face_dn, jnp.float32) / area
        w_up = jnp.where(index == total - 1, 0.0, w_up)
        w_dn = jnp.where(index == 0, 0.0, w_dn)
        before = halo[0, t]
        after = halo[1, t]
        q = [[st[f, row + 1, at, h * LANES : (h + 1) * LANES] for h in range(2)] for f in range(FIELDS)]
        back, ahead = [], []
        for f in range(FIELDS):
            k = f * rows + row
            b = pltpu.roll(before, (LANES - k) % LANES, 1)
            a = pltpu.roll(after, LANES - 1 - k, 1)
            low, high = q[f]
            low_r, high_r = pltpu.roll(low, 1, 1), pltpu.roll(high, 1, 1)
            low_l, high_l = pltpu.roll(low, LANES - 1, 1), pltpu.roll(high, LANES - 1, 1)
            back.append([jnp.where(lane == 0, b, low_r), jnp.where(lane == 0, low_r, high_r)])
            ahead.append(
                [jnp.where(lane == LANES - 1, high_l, low_l), jnp.where(lane == LANES - 1, a, high_l)]
            )
        for h in range(2):
            cols = slice(h * LANES, (h + 1) * LANES)
            c = [q[f][h] for f in range(FIELDS)]
            inner = [st[f, row, at, cols] for f in range(FIELDS)]
            outer = [st[f, row + 2, at, cols] for f in range(FIELDS)]
            above, below = [], []
            for f in range(FIELDS):
                prev = st[f, row + 1, at_dn, cols]
                nxt = st[f, row + 1, at_up, cols]
                below.append(pltpu.roll(jnp.where(sub == SUB - 1, prev, c[f]), 1, 0))
                above.append(pltpu.roll(jnp.where(sub == 0, nxt, c[f]), SUB - 1, 0))
            below[4] = jnp.where(t0 + sub == 0, c[4], below[4])
            above[4] = jnp.where(t0 + sub == tiles * SUB - 1, c[4], above[4])
            inv = 1.0 / c[0]
            v_r, v_p, v_t = c[1] * inv, c[2] * inv, c[3] * inv
            r_up = 0.5 * (v_r + outer[1] / outer[0])
            r_dn = 0.5 * (v_r + inner[1] / inner[0])
            p_up = 0.5 * (v_p + ahead[2][h] / ahead[0][h])
            p_dn = 0.5 * (v_p + back[2][h] / back[0][h])
            t_up_v = jnp.where(t0 + sub == tiles * SUB - 1, 0.0, 0.5 * (v_t + above[3] / above[0]))
            t_dn_v = jnp.where(t0 + sub == 0, 0.0, 0.5 * (v_t + below[3] / below[0]))
            r_up_w, r_dn_w = r_up * w_up, r_dn * w_dn
            for f in range(FIELDS):
                out = c[f]
                out -= r_up_w * jnp.where(r_up > 0, c[f], outer[f]) - r_dn_w * jnp.where(r_dn > 0, inner[f], c[f])
                out -= upwind(t_up_v, c[f], above[f]) - upwind(t_dn_v, below[f], c[f])
                out -= upwind(p_up, c[f], ahead[f][h]) - upwind(p_dn, back[f][h], c[f])
                if f == 1:
                    out -= 0.5 * (0.5 * (0.4 * outer[4] - 0.4 * inner[4]))
                if f == 2:
                    out -= 0.5 * (0.5 * (0.4 * ahead[4][h] - 0.4 * back[4][h]))
                if f == 3:
                    out -= 0.5 * (0.5 * (0.4 * above[4] - 0.4 * below[4]))
                send[row, t, h, f] = out

    def whole_row(row, c):
        lax.fori_loop(0, per, lambda p, _: (compute(row, c * per + p), 0)[1], 0)

    def first_leg(c, row):
        part = send.at[row, pl.ds(c * per, per)]
        return part, whole[c].at[me]

    def produce(c, wanted):
        def step(k, _):
            row = peer(me, k)

            def do():
                whole_row(row, c)
                part, place = first_leg(c, row)

                @pl.when(row != me)
                def _():
                    remote(part, place, s1.at[c], r1.at[c], az=row).start()

                @pl.when(row == me)
                def _():
                    pltpu.make_async_copy(part, place, own1.at[c]).start()

            edge = (row == 0) | (row == rows - 1)
            if wanted == "all":
                do()
            elif wanted == "edge":
                pl.when(edge)(do)
            else:
                pl.when(jnp.logical_not(edge))(do)
            return 0

        lax.fori_loop(0, rows, step, 0)

    right.wait()
    left.wait()
    for c in range(early):
        produce(c, "inside")

    @pl.when(jnp.logical_not(at_inner))
    def _():
        for c in outward:
            c.wait_recv()

    @pl.when(jnp.logical_not(at_outer))
    def _():
        for c in inward:
            c.wait_recv()

    @pl.when(at_inner)
    def _():
        st[:, 0] = st[:, 1]

    @pl.when(at_outer)
    def _():
        st[:, rows + 1] = st[:, rows]

    for c in range(early):
        produce(c, "edge")
    for c in range(early, chunks):
        produce(c, "all")

    amount = amounts[me]
    skip = amount // LANES
    turn = amount % LANES

    def second_leg(c, b):
        thetas = pl.ds(c * per * SUB, per * SUB)
        return turned.at[b, :, thetas], landed.at[me, :, thetas]

    for c in range(chunks):
        wait_bytes(whole[c].at[pl.ds(0, n - 1)], r1.at[c])
        pltpu.make_async_copy(send.at[me, pl.ds(c * per, per)], whole[c].at[me], own1.at[c]).wait()

        def give(k, _, c=c):
            b = peer(me, k)
            for h in range(2):
                a = (2 * b + h - skip) & (2 * n - 1)
                z = (2 * b + h - skip - 1) & (2 * n - 1)
                for p in range(per):
                    for f in range(FIELDS):
                        late = pltpu.roll(whole[c][a // 2, p, a % 2, f], turn, 1)
                        soon = pltpu.roll(whole[c][z // 2, p, z % 2, f], turn, 1)
                        value = jnp.where(lane >= turn, late, soon)
                        turned[b, f, pl.ds((c * per + p) * SUB, SUB), h * LANES : (h + 1) * LANES] = value

            src, dst = second_leg(c, b)

            @pl.when(b != me)
            def _():
                remote(src, dst, s2, r2, az=b).start()

            @pl.when(b == me)
            def _():
                pltpu.make_async_copy(src, dst, own2).start()

            return 0

        lax.fori_loop(0, n, give, 0)

    for c in range(chunks):
        wait_bytes(send.at[pl.ds(0, n - 1), pl.ds(c * per, per)], s1.at[c])
    wait_bytes(landed.at[pl.ds(0, n - 1)], s2)
    wait_bytes(landed.at[me], own2)
    wait_bytes(landed.at[pl.ds(0, n - 1)], r2)

    @pl.when(jnp.logical_not(at_outer))
    def _():
        for c in outward:
            c.wait_send()

    @pl.when(jnp.logical_not(at_inner))
    def _():
        for c in inward:
            c.wait_send()


def deliver(landed, den_o, mom_o, en_o, sems):
    rows = den_o.shape[0]
    parts = sems.shape[0]
    copies = []
    for p in range(parts):
        at = pl.ds(p * (rows // parts), rows // parts)
        copies.append(pltpu.make_async_copy(landed.at[at, 0], den_o.at[at], sems.at[p, 0]))
        for f in range(3):
            copies.append(pltpu.make_async_copy(landed.at[at, 1 + f], mom_o.at[f, at], sems.at[p, 1 + f]))
        copies.append(pltpu.make_async_copy(landed.at[at, 4], en_o.at[at], sems.at[p, 4]))
    for c in copies:
        c.start()
    for c in copies:
        c.wait()


def per_device(density, momenta, energy, shifts):
    rows, thetas, width = density.shape
    n = lax.axis_size("az")
    tiles = thetas // SUB
    chunks, early = 8, 2
    per = tiles // chunks
    dma = pltpu.SemaphoreType.DMA
    f32 = jnp.float32
    hbm = pl.BlockSpec(memory_space=pltpu.HBM)
    landed = pl.pallas_call(
        functools.partial(kernel, chunks, early),
        out_shape=pltpu.VMEM((n, FIELDS, thetas, width), f32),
        in_specs=[hbm] * 4,
        out_specs=pl.BlockSpec(memory_space=pltpu.VMEM),
        scratch_shapes=[
            pltpu.SMEM((rows,), jnp.int32),
            pltpu.VMEM((FIELDS, rows + 2, thetas, width), f32),
            pltpu.VMEM((rows, tiles, 2, FIELDS, SUB, LANES), f32),
            pltpu.VMEM((n, FIELDS, thetas, width), f32),
            pltpu.VMEM((2, tiles, SUB, LANES), f32),
            pltpu.VMEM((2, tiles, SUB, LANES), f32),
            *[pltpu.VMEM((n, per, 2, FIELDS, SUB, LANES), f32) for _ in range(chunks)],
            dma((4,)),
            dma((2, 3)),
            dma((2, 3)),
            dma((2,)),
            dma((2,)),
            dma((chunks,)),
            dma((chunks,)),
            dma((chunks,)),
            dma,
            dma,
            dma,
        ],
        compiler_params=pltpu.CompilerParams(
            collective_id=0, has_side_effects=True, vmem_limit_bytes=56 * 2**20
        ),
        name="transport",
    )(density, momenta, energy, shifts)
    return pl.pallas_call(
        deliver,
        out_shape=[jax.ShapeDtypeStruct(x.shape, f32) for x in (density, momenta, energy)],
        in_specs=[pl.BlockSpec(memory_space=pl.ANY)],
        out_specs=[pl.BlockSpec(memory_space=pl.ANY)] * 3,
        scratch_shapes=[dma((4, FIELDS))],
        compiler_params=pltpu.CompilerParams(vmem_limit_bytes=2**20),
        name="deliver",
    )(landed)


def solution(mesh):
    return jax.shard_map(
        per_device,
        mesh=mesh,
        in_specs=(P("rad", None, "az"), P(None, "rad", None, "az"), P("rad", None, "az"), P("rad")),
        out_specs=(P("rad", None, "az"), P(None, "rad", None, "az"), P("rad", None, "az")),
        check_vma=False,
    )
```

time: 683 us -> 138 us (0.20)
  the two profiles are of different devices: /device:TPU:65 before, /device:TPU:22 now
where the time goes in v1:
time: 138 us
  Pallas kernels  138 us (100%)
    pallas_call x1, Pallas kernels, per_device(): pl.pallas_call(functools.partial(kernel, chunks, early), out_shape=pltpu....  135 us

profile of v1, /device:TPU:22, one launch (start us, length us, event | category | flops | bytes accessed | tf_op | source)
XLA Modules:
  0.0 138.2 jit_solution(7395130790341853625)
XLA Ops:
  0.6 135.1 %transport.1.landed = f32[16,5,64,256]{3,2,1,0:T(8,128)S(1)} custom-call(f32[16,64,256]{2,1,0:T(8,128)} %den.1, f32[3,16,64,256]{3,2,1,0:T(8,128)} %mom.1, f32[16,64,256]{2,1,0:T(8,128)} %en.1, s32[16]{0:T(128)} %shifts.1), custom_call_target="tpu_custom_call" | custom-call | tf_op jit(solution)/shard_map/transport/pallas_call | solution.py:336
  135.7 2.5 %deliver.1 = (f32[16,64,256]{2,1,0:T(8,128)}, f32[3,16,64,256]{3,2,1,0:T(8,128)}, f32[16,64,256]{2,1,0:T(8,128)}) custom-call(f32[16,5,64,256]{3,2,1,0:T(8,128)S(1)} %transport.1.landed), custom_call_target="tpu_custom_call" | custom-call | tf_op jit(solution)/shard_map/deliver/pallas_call | solution.py:366

commit v2 on v1

--- a/solution.py
+++ b/solution.py
@@ -31,9 +31,9 @@
 
 
 def kernel(chunks, early, den, mom, en, shifts, landed, *refs):
-    amounts, st, send, turned, pack, halo = refs[:6]
-    whole = refs[6 : 6 + chunks]
-    in_sem, rad_send, rad_recv, az_send, az_recv, s1, r1, own1, s2, r2, own2 = refs[6 + chunks :]
+    amounts, st, send, turned, pack, halo, relay = refs[:7]
+    whole = refs[7 : 7 + chunks]
+    in_sem, shift_sem, rad_send, rad_recv, relay_send, relay_recv, az_send, az_recv, s1, r1, own1, s2, r2, own2 = refs[7 + chunks :]
     rows = den.shape[0]
     tiles = den.shape[1] // SUB
     per = tiles // chunks
@@ -44,14 +44,20 @@
     at_inner = pos == 0
     at_outer = pos == groups - 1
 
-    loads = [
-        pltpu.make_async_copy(den, st.at[0, pl.ds(1, rows)], in_sem.at[0]),
-        pltpu.make_async_copy(mom, st.at[pl.ds(1, 3), pl.ds(1, rows)], in_sem.at[1]),
-        pltpu.make_async_copy(en, st.at[4, pl.ds(1, rows)], in_sem.at[2]),
-        pltpu.make_async_copy(shifts, amounts, in_sem.at[3]),
-    ]
-    for c in loads:
-        c.start()
+    def load(j, first, count):
+        at = pl.ds(first * SUB, count * SUB)
+        return [
+            pltpu.make_async_copy(den.at[:, at], st.at[0, pl.ds(1, rows), at], in_sem.at[j, 0]),
+            pltpu.make_async_copy(mom.at[:, :, at], st.at[pl.ds(1, 3), pl.ds(1, rows), at], in_sem.at[j, 1]),
+            pltpu.make_async_copy(en.at[:, at], st.at[4, pl.ds(1, rows), at], in_sem.at[j, 2]),
+        ]
+
+    loads = [load(0, 0, 2), load(1, 2, tiles - 2)]
+    get_shifts = pltpu.make_async_copy(shifts, amounts, shift_sem)
+    for part in loads:
+        for c in part:
+            c.start()
+    get_shifts.start()
 
     barrier = pltpu.get_barrier_semaphore()
 
@@ -61,39 +67,120 @@
 
     lax.fori_loop(1, n, greet, 0)
 
-    @pl.when(jnp.logical_not(at_outer))
-    def _():
-        pl.semaphore_signal(barrier, 1, device_id={"rad": pos + 1}, device_id_type=MESH)
-
-    @pl.when(jnp.logical_not(at_inner))
-    def _():
-        pl.semaphore_signal(barrier, 1, device_id={"rad": pos - 1}, device_id_type=MESH)
-
-    apart = jnp.where(at_inner, 0, 1) + jnp.where(at_outer, 0, 1)
-    pl.semaphore_wait(barrier, n - 1 + apart)
-
-    def radial(row, slot, way, to):
-        return [
-            remote(den.at[row], st.at[0, slot], rad_send.at[way, 0], rad_recv.at[way, 0], rad=to),
-            remote(mom.at[:, row], st.at[pl.ds(1, 3), slot], rad_send.at[way, 1], rad_recv.at[way, 1], rad=to),
-            remote(en.at[row], st.at[4, slot], rad_send.at[way, 2], rad_recv.at[way, 2], rad=to),
-        ]
-
-    outward = radial(rows - 1, 0, 0, (pos + 1) % groups)
-    inward = radial(0, rows + 1, 1, (pos + groups - 1) % groups)
-
-    @pl.when(jnp.logical_not(at_outer))
+    for j in range(1, groups):
+        pl.semaphore_signal(barrier, 1, device_id={"rad": (pos + j) % groups}, device_id_type=MESH)
+    pl.semaphore_wait(barrier, n - 1 + groups - 1)
+
+    half = groups // 2
+    part_rows = tiles * SUB // half
+
+    def edge_part(row, p):
+        at = pl.ds(p * part_rows, part_rows)
+        return [den.at[row, at], mom.at[:, row, at], en.at[row, at]]
+
+    def slot_part(slot, p):
+        at = pl.ds(p * part_rows, part_rows)
+        return [st.at[0, slot, at], st.at[pl.ds(1, 3), slot, at], st.at[4, slot, at]]
+
+    def relay_part():
+        return [relay.at[0], relay.at[pl.ds(1, 3)], relay.at[4]]
+
+    def copies(srcs, dsts, send, recv, to):
+        return [remote(a, b, send.at[j], recv.at[j], rad=to) for j, (a, b) in enumerate(zip(srcs, dsts))]
+
+    def radial(way, row, slot, to):
+        whole_edge = [den.at[row], mom.at[:, row], en.at[row]]
+        return copies(whole_edge, [st.at[0, slot], st.at[pl.ds(1, 3), slot], st.at[4, slot]],
+                      rad_send.at[way, 0], rad_recv.at[way, 0], to)
+
+    outward = radial(0, rows - 1, 0, (pos + 1) % groups)
+    inward = radial(1, 0, rows + 1, (pos + groups - 1) % groups)
+    seams = []
+    for way, row, slot, source, target, first in ((0, rows - 1, 0, half - 1, half, 0), (1, 0, rows + 1, half, half - 1, half)):
+        seam = []
+        for p in range(half):
+            via = first + p
+            final = (slot_part(slot, p), rad_recv.at[way, p], target)
+            if via == source:
+                seam.append((via, copies(edge_part(row, p), final[0], rad_send.at[way, p], final[1], target), None))
+            else:
+                to_relay = copies(edge_part(row, p), relay_part(), rad_send.at[way, p], relay_recv, via)
+                from_relay = copies(relay_part(), final[0], relay_send, final[1], target)
+                seam.append((via, to_relay, from_relay))
+        seams.append((source, target, seam))
+
+    has_out = jnp.logical_not(at_outer) & (pos != half - 1)
+    has_in = jnp.logical_not(at_inner) & (pos != half)
+
+    @pl.when(has_out)
     def _():
         for c in outward:
             c.start()
 
-    @pl.when(jnp.logical_not(at_inner))
+    @pl.when(has_in)
     def _():
         for c in inward:
             c.start()
 
-    for c in loads:
-        c.wait()
+    for source, target, seam in seams:
+        @pl.when(pos == source)
+        def _():
+            for via, leg, _ in seam:
+                for c in leg:
+                    c.start()
+
+    def forward():
+        for source, target, seam in seams:
+            for via, leg, onward in seam:
+                if onward is not None:
+                    @pl.when(pos == via)
+                    def _():
+                        for a, b in zip(leg, onward):
+                            a.wait_recv()
+                            b.start()
+
+    def radial_arrived():
+        @pl.when(jnp.logical_not(at_inner) & (pos != half))
+        def _():
+            for c in outward:
+                c.wait_recv()
+
+        @pl.when(jnp.logical_not(at_outer) & (pos != half - 1))
+        def _():
+            for c in inward:
+                c.wait_recv()
+
+        for source, target, seam in seams:
+            @pl.when(pos == target)
+            def _():
+                for via, leg, onward in seam:
+                    for c in onward or leg:
+                        c.wait_recv()
+
+    def radial_sent():
+        @pl.when(has_out)
+        def _():
+            for c in outward:
+                c.wait_send()
+
+        @pl.when(has_in)
+        def _():
+            for c in inward:
+                c.wait_send()
+
+        for source, target, seam in seams:
+            @pl.when(pos == source)
+            def _():
+                for via, leg, onward in seam:
+                    for c in leg:
+                        c.wait_send()
+
+            for via, leg, onward in seam:
+                if onward is not None:
+                    @pl.when(pos == via)
+                    def _():
+                        for c in onward:
+                            c.wait_send()
 
     lane = lax.broadcasted_iota(jnp.int32, (SUB, LANES), 1)
     sub = lax.broadcasted_iota(jnp.int32, (SUB, LANES), 0)
@@ -113,13 +200,27 @@
         pack[1, t] = last
         return 0
 
-    lax.fori_loop(0, tiles, packing, 0)
-    right = remote(pack.at[1], halo.at[0], az_send.at[0], az_recv.at[0], az=(me + 1) % n)
-    left = remote(pack.at[0], halo.at[1], az_send.at[1], az_recv.at[1], az=(me + n - 1) % n)
-    right.start()
-    left.start()
-
-    total = (groups * rows)
+    def edges(j, first, count):
+        at = pl.ds(first, count)
+        return [
+            remote(pack.at[1, at], halo.at[0, at], az_send.at[j, 0], az_recv.at[j, 0], az=(me + 1) % n),
+            remote(pack.at[0, at], halo.at[1, at], az_send.at[j, 1], az_recv.at[j, 1], az=(me + n - 1) % n),
+        ]
+
+    azimuthal = [edges(0, 0, 1), edges(1, 1, tiles - 1)]
+    for c in loads[0]:
+        c.wait()
+    packing(0, 0)
+    for c in azimuthal[0]:
+        c.start()
+    for c in loads[1]:
+        c.wait()
+    lax.fori_loop(1, tiles, packing, 0)
+    for c in azimuthal[1]:
+        c.start()
+    get_shifts.wait()
+
+    total = groups * rows
 
     def radius(index):
         return 1.0 + 2.0 * (index.astype(jnp.float32) + 0.5) / total
@@ -225,20 +326,16 @@
 
         lax.fori_loop(0, rows, step, 0)
 
-    right.wait()
-    left.wait()
-    for c in range(early):
+    for c in azimuthal[0]:
+        c.wait()
+    produce(0, "inside")
+    forward()
+    for c in azimuthal[1]:
+        c.wait()
+    for c in range(1, early):
         produce(c, "inside")
 
-    @pl.when(jnp.logical_not(at_inner))
-    def _():
-        for c in outward:
-            c.wait_recv()
-
-    @pl.when(jnp.logical_not(at_outer))
-    def _():
-        for c in inward:
-            c.wait_recv()
+    radial_arrived()
 
     @pl.when(at_inner)
     def _():
@@ -297,15 +394,7 @@
     wait_bytes(landed.at[me], own2)
     wait_bytes(landed.at[pl.ds(0, n - 1)], r2)
 
-    @pl.when(jnp.logical_not(at_outer))
-    def _():
-        for c in outward:
-            c.wait_send()
-
-    @pl.when(jnp.logical_not(at_inner))
-    def _():
-        for c in inward:
-            c.wait_send()
+    radial_sent()
 
 
 def deliver(landed, den_o, mom_o, en_o, sems):
@@ -330,6 +419,7 @@
     tiles = thetas // SUB
     chunks, early = 8, 2
     per = tiles // chunks
+    half = lax.axis_size("rad") // 2
     dma = pltpu.SemaphoreType.DMA
     f32 = jnp.float32
     hbm = pl.BlockSpec(memory_space=pltpu.HBM)
@@ -345,12 +435,16 @@
             pltpu.VMEM((n, FIELDS, thetas, width), f32),
             pltpu.VMEM((2, tiles, SUB, LANES), f32),
             pltpu.VMEM((2, tiles, SUB, LANES), f32),
+            pltpu.VMEM((FIELDS, 2 * thetas // lax.axis_size("rad"), width), f32),
             *[pltpu.VMEM((n, per, 2, FIELDS, SUB, LANES), f32) for _ in range(chunks)],
-            dma((4,)),
             dma((2, 3)),
-            dma((2, 3)),
-            dma((2,)),
-            dma((2,)),
+            dma,
+            dma((2, half, 3)),
+            dma((2, half, 3)),
+            dma((3,)),
+            dma((3,)),
+            dma((2, 2)),
+            dma((2, 2)),
             dma((chunks,)),
             dma((chunks,)),
             dma((chunks,)),

time: 138 us -> 137 us (level)
  the two profiles are of different devices: /device:TPU:22 before, /device:TPU:1 now
where the time goes in v2:
time: 137 us; the launch traced here: 136 us
  Pallas kernels  136 us (99%)
    pallas_call x1, Pallas kernels, per_device(): pl.pallas_call(functools.partial(kernel, chunks, early), out_shape=pltpu....  133 us

profile of v2, /device:TPU:1, one launch (start us, length us, event | category | flops | bytes accessed | tf_op | source)
XLA Modules:
  0.0 136.5 jit_solution(13962472445332523652)
XLA Ops:
  0.6 133.3 %transport.1.landed = f32[16,5,64,256]{3,2,1,0:T(8,128)S(1)} custom-call(f32[16,64,256]{2,1,0:T(8,128)} %den.1, f32[3,16,64,256]{3,2,1,0:T(8,128)} %mom.1, f32[16,64,256]{2,1,0:T(8,128)} %en.1, s32[16]{0:T(128)} %shifts.1), custom_call_target="tpu_custom_call" | custom-call | tf_op jit(solution)/shard_map/transport/pallas_call | solution.py:426
  134.0 2.5 %deliver.1 = (f32[16,64,256]{2,1,0:T(8,128)}, f32[3,16,64,256]{3,2,1,0:T(8,128)}, f32[16,64,256]{2,1,0:T(8,128)}) custom-call(f32[16,5,64,256]{3,2,1,0:T(8,128)S(1)} %transport.1.landed), custom_call_target="tpu_custom_call" | custom-call | tf_op jit(solution)/shard_map/deliver/pallas_call | solution.py:460

commit v3 on v2

--- a/solution.py
+++ b/solution.py
@@ -67,50 +67,29 @@
 
     lax.fori_loop(1, n, greet, 0)
 
-    for j in range(1, groups):
-        pl.semaphore_signal(barrier, 1, device_id={"rad": (pos + j) % groups}, device_id_type=MESH)
-    pl.semaphore_wait(barrier, n - 1 + groups - 1)
-
     half = groups // 2
-    part_rows = tiles * SUB // half
-
-    def edge_part(row, p):
-        at = pl.ds(p * part_rows, part_rows)
-        return [den.at[row, at], mom.at[:, row, at], en.at[row, at]]
-
-    def slot_part(slot, p):
-        at = pl.ds(p * part_rows, part_rows)
-        return [st.at[0, slot, at], st.at[pl.ds(1, 3), slot, at], st.at[4, slot, at]]
-
-    def relay_part():
-        return [relay.at[0], relay.at[pl.ds(1, 3)], relay.at[4]]
-
-    def copies(srcs, dsts, send, recv, to):
-        return [remote(a, b, send.at[j], recv.at[j], rad=to) for j, (a, b) in enumerate(zip(srcs, dsts))]
+    across = (pos + half) % groups
+    has_out = jnp.logical_not(at_outer) & (pos != half - 1)
+    has_in = jnp.logical_not(at_inner) & (pos != half)
+    pl.semaphore_signal(barrier, 1, device_id={"rad": across}, device_id_type=MESH)
+
+    @pl.when(has_out)
+    def _():
+        pl.semaphore_signal(barrier, 1, device_id={"rad": pos + 1}, device_id_type=MESH)
+
+    @pl.when(has_in)
+    def _():
+        pl.semaphore_signal(barrier, 1, device_id={"rad": pos - 1}, device_id_type=MESH)
+
+    pl.semaphore_wait(barrier, n + jnp.where(has_out, 1, 0) + jnp.where(has_in, 1, 0))
 
     def radial(way, row, slot, to):
-        whole_edge = [den.at[row], mom.at[:, row], en.at[row]]
-        return copies(whole_edge, [st.at[0, slot], st.at[pl.ds(1, 3), slot], st.at[4, slot]],
-                      rad_send.at[way, 0], rad_recv.at[way, 0], to)
+        srcs = [den.at[row], mom.at[:, row], en.at[row]]
+        dsts = [st.at[0, slot], st.at[pl.ds(1, 3), slot], st.at[4, slot]]
+        return [remote(a, b, rad_send.at[way, j], rad_recv.at[way, j], rad=to) for j, (a, b) in enumerate(zip(srcs, dsts))]
 
     outward = radial(0, rows - 1, 0, (pos + 1) % groups)
     inward = radial(1, 0, rows + 1, (pos + groups - 1) % groups)
-    seams = []
-    for way, row, slot, source, target, first in ((0, rows - 1, 0, half - 1, half, 0), (1, 0, rows + 1, half, half - 1, half)):
-        seam = []
-        for p in range(half):
-            via = first + p
-            final = (slot_part(slot, p), rad_recv.at[way, p], target)
-            if via == source:
-                seam.append((via, copies(edge_part(row, p), final[0], rad_send.at[way, p], final[1], target), None))
-            else:
-                to_relay = copies(edge_part(row, p), relay_part(), rad_send.at[way, p], relay_recv, via)
-                from_relay = copies(relay_part(), final[0], relay_send, final[1], target)
-                seam.append((via, to_relay, from_relay))
-        seams.append((source, target, seam))
-
-    has_out = jnp.logical_not(at_outer) & (pos != half - 1)
-    has_in = jnp.logical_not(at_inner) & (pos != half)
 
     @pl.when(has_out)
     def _():
@@ -122,40 +101,70 @@
         for c in inward:
             c.start()
 
-    for source, target, seam in seams:
-        @pl.when(pos == source)
-        def _():
-            for via, leg, _ in seam:
-                for c in leg:
-                    c.start()
-
-    def forward():
-        for source, target, seam in seams:
-            for via, leg, onward in seam:
-                if onward is not None:
-                    @pl.when(pos == via)
-                    def _():
-                        for a, b in zip(leg, onward):
-                            a.wait_recv()
-                            b.start()
+    part_rows = tiles * SUB // half
+    low = pos < half
+    place = pos % half
+
+    def seam_part(way, p):
+        carries = jnp.where(low, p <= place, p >= place)
+        crossing = low if way == 0 else jnp.logical_not(low)
+        step = groups - 1 if way == 0 else 1
+        to = jnp.where(crossing & (p == place), across, (pos + step) % groups)
+        last = pos == (half if way == 0 else half - 1)
+        at = pl.ds(p * part_rows, part_rows)
+        edge = st.at[:, rows if way == 0 else 1, at]
+
+        def copy(src):
+            return remote(src, relay.at[way, p], relay_send.at[way, p], relay_recv.at[way, p], rad=to)
+
+        return carries, carries & jnp.logical_not(last), copy, edge
+
+    def seam(stage):
+        for way in range(2):
+            hops = jnp.where(low, half - 1 - place, half - place) if way == 0 else jnp.where(low, place + 1, place)
+
+            @pl.when(hops == stage)
+            def _():
+                for p in range(half):
+                    carries, hands_on, copy, edge = seam_part(way, p)
+                    if stage == 0:
+                        @pl.when(carries)
+                        def _():
+                            copy(edge).start()
+                    else:
+                        @pl.when(carries)
+                        def _():
+                            copy(relay.at[way, p]).wait_recv()
+
+                        @pl.when(hands_on)
+                        def _():
+                            copy(relay.at[way, p]).start()
+
+    def seam_into_state():
+        for way in range(2):
+            @pl.when(pos == (half if way == 0 else half - 1))
+            def _():
+                for p in range(half):
+                    st[:, 0 if way == 0 else rows + 1, p * part_rows : (p + 1) * part_rows] = relay[way, p]
 
     def radial_arrived():
-        @pl.when(jnp.logical_not(at_inner) & (pos != half))
+        @pl.when(has_in)
         def _():
             for c in outward:
                 c.wait_recv()
 
-        @pl.when(jnp.logical_not(at_outer) & (pos != half - 1))
+        @pl.when(has_out)
         def _():
             for c in inward:
                 c.wait_recv()
 
-        for source, target, seam in seams:
-            @pl.when(pos == target)
-            def _():
-                for via, leg, onward in seam:
-                    for c in onward or leg:
-                        c.wait_recv()
+        @pl.when(at_inner)
+        def _():
+            st[:, 0] = st[:, 1]
+
+        @pl.when(at_outer)
+        def _():
+            st[:, rows + 1] = st[:, rows]
 
     def radial_sent():
         @pl.when(has_out)
@@ -168,19 +177,13 @@
             for c in inward:
                 c.wait_send()
 
-        for source, target, seam in seams:
-            @pl.when(pos == source)
-            def _():
-                for via, leg, onward in seam:
-                    for c in leg:
-                        c.wait_send()
-
-            for via, leg, onward in seam:
-                if onward is not None:
-                    @pl.when(pos == via)
-                    def _():
-                        for c in onward:
-                            c.wait_send()
+        for way in range(2):
+            for p in range(half):
+                carries, hands_on, copy, edge = seam_part(way, p)
+
+                @pl.when(hands_on)
+                def _():
+                    copy(relay.at[way, p]).wait_send()
 
     lane = lax.broadcasted_iota(jnp.int32, (SUB, LANES), 1)
     sub = lax.broadcasted_iota(jnp.int32, (SUB, LANES), 0)
@@ -215,6 +218,7 @@
         c.start()
     for c in loads[1]:
         c.wait()
+    seam(0)
     lax.fori_loop(1, tiles, packing, 0)
     for c in azimuthal[1]:
         c.start()
@@ -295,30 +299,34 @@
     def whole_row(row, c):
         lax.fori_loop(0, per, lambda p, _: (compute(row, c * per + p), 0)[1], 0)
 
+    def turn_of(c):
+        return c * rows // early % rows
+
     def first_leg(c, row):
         part = send.at[row, pl.ds(c * per, per)]
         return part, whole[c].at[me]
 
     def produce(c, wanted):
         def step(k, _):
-            row = peer(me, k)
+            to = peer(me, k)
+            row = (to + n - turn_of(c)) % n
 
             def do():
                 whole_row(row, c)
                 part, place = first_leg(c, row)
 
-                @pl.when(row != me)
+                @pl.when(to != me)
                 def _():
-                    remote(part, place, s1.at[c], r1.at[c], az=row).start()
-
-                @pl.when(row == me)
+                    remote(part, place, s1.at[c], r1.at[c], az=to).start()
+
+                @pl.when(to == me)
                 def _():
                     pltpu.make_async_copy(part, place, own1.at[c]).start()
 
             edge = (row == 0) | (row == rows - 1)
-            if wanted == "all":
+            if wanted == "every":
                 do()
-            elif wanted == "edge":
+            elif wanted == "edges":
                 pl.when(edge)(do)
             else:
                 pl.when(jnp.logical_not(edge))(do)
@@ -328,41 +336,32 @@
 
     for c in azimuthal[0]:
         c.wait()
-    produce(0, "inside")
-    forward()
-    for c in azimuthal[1]:
-        c.wait()
-    for c in range(1, early):
-        produce(c, "inside")
-
-    radial_arrived()
-
-    @pl.when(at_inner)
-    def _():
-        st[:, 0] = st[:, 1]
-
-    @pl.when(at_outer)
-    def _():
-        st[:, rows + 1] = st[:, rows]
-
-    for c in range(early):
-        produce(c, "edge")
-    for c in range(early, chunks):
-        produce(c, "all")
-
-    amount = amounts[me]
-    skip = amount // LANES
-    turn = amount % LANES
+    for c in range(chunks):
+        produce(c, "inside" if c < early else "every")
+        if c == 0:
+            for a in azimuthal[1]:
+                a.wait()
+        if c < half:
+            seam(c + 1)
+        if c == early - 1:
+            radial_arrived()
+            seam_into_state()
+            for e in range(early):
+                produce(e, "edges")
 
     def second_leg(c, b):
         thetas = pl.ds(c * per * SUB, per * SUB)
-        return turned.at[b, :, thetas], landed.at[me, :, thetas]
+        return turned.at[b, :, thetas], landed.at[(me + n - turn_of(c)) % n, :, thetas]
 
     for c in range(chunks):
         wait_bytes(whole[c].at[pl.ds(0, n - 1)], r1.at[c])
         pltpu.make_async_copy(send.at[me, pl.ds(c * per, per)], whole[c].at[me], own1.at[c]).wait()
 
-        def give(k, _, c=c):
+        amount = amounts[(me + n - turn_of(c)) % n]
+        skip = amount // LANES
+        turn = amount % LANES
+
+        def give(k, _, c=c, skip=skip, turn=turn):
             b = peer(me, k)
             for h in range(2):
                 a = (2 * b + h - skip) & (2 * n - 1)
@@ -417,7 +416,7 @@
     rows, thetas, width = density.shape
     n = lax.axis_size("az")
     tiles = thetas // SUB
-    chunks, early = 8, 2
+    chunks, early = 8, 4
     per = tiles // chunks
     half = lax.axis_size("rad") // 2
     dma = pltpu.SemaphoreType.DMA
@@ -435,14 +434,14 @@
             pltpu.VMEM((n, FIELDS, thetas, width), f32),
             pltpu.VMEM((2, tiles, SUB, LANES), f32),
             pltpu.VMEM((2, tiles, SUB, LANES), f32),
-            pltpu.VMEM((FIELDS, 2 * thetas // lax.axis_size("rad"), width), f32),
+            pltpu.VMEM((2, half, FIELDS, thetas // half, width), f32),
             *[pltpu.VMEM((n, per, 2, FIELDS, SUB, LANES), f32) for _ in range(chunks)],
             dma((2, 3)),
             dma,
-            dma((2, half, 3)),
-            dma((2, half, 3)),
-            dma((3,)),
-            dma((3,)),
+            dma((2, 3)),
+            dma((2, 3)),
+            dma((2, half)),
+            dma((2, half)),
             dma((2, 2)),
             dma((2, 2)),
             dma((chunks,)),

time: 137 us -> 135 us (0.985)
  the two profiles are of different devices: /device:TPU:1 before, /device:TPU:65 now
where the time goes in v3:
time: 135 us
  Pallas kernels  134 us (99%)
    pallas_call x1, Pallas kernels, per_device(): pl.pallas_call(functools.partial(kernel, chunks, early), out_shape=pltpu....  131 us

profile of v3, /device:TPU:65, one launch (start us, length us, event | category | flops | bytes accessed | tf_op | source)
XLA Modules:
  0.0 134.5 jit_solution(6917598898215548750)
XLA Ops:
  0.6 131.4 %transport.1.landed = f32[16,5,64,256]{3,2,1,0:T(8,128)S(1)} custom-call(f32[16,64,256]{2,1,0:T(8,128)} %den.1, f32[3,16,64,256]{3,2,1,0:T(8,128)} %mom.1, f32[16,64,256]{2,1,0:T(8,128)} %en.1, s32[16]{0:T(128)} %shifts.1), custom_call_target="tpu_custom_call" | custom-call | tf_op jit(solution)/shard_map/transport/pallas_call | solution.py:425
  132.0 2.5 %deliver.1 = (f32[16,64,256]{2,1,0:T(8,128)}, f32[3,16,64,256]{3,2,1,0:T(8,128)}, f32[16,64,256]{2,1,0:T(8,128)}) custom-call(f32[16,5,64,256]{3,2,1,0:T(8,128)S(1)} %transport.1.landed), custom_call_target="tpu_custom_call" | custom-call | tf_op jit(solution)/shard_map/deliver/pallas_call | solution.py:459

commit v4 on v3

--- a/solution.py
+++ b/solution.py
@@ -91,16 +91,6 @@
     outward = radial(0, rows - 1, 0, (pos + 1) % groups)
     inward = radial(1, 0, rows + 1, (pos + groups - 1) % groups)
 
-    @pl.when(has_out)
-    def _():
-        for c in outward:
-            c.start()
-
-    @pl.when(has_in)
-    def _():
-        for c in inward:
-            c.start()
-
     part_rows = tiles * SUB // half
     low = pos < half
     place = pos % half
@@ -112,12 +102,15 @@
         to = jnp.where(crossing & (p == place), across, (pos + step) % groups)
         last = pos == (half if way == 0 else half - 1)
         at = pl.ds(p * part_rows, part_rows)
-        edge = st.at[:, rows if way == 0 else 1, at]
-
-        def copy(src):
-            return remote(src, relay.at[way, p], relay_send.at[way, p], relay_recv.at[way, p], rad=to)
-
-        return carries, carries & jnp.logical_not(last), copy, edge
+        row = rows - 1 if way == 0 else 0
+        edge = [den.at[row, at], mom.at[:, row, at], en.at[row, at]]
+        slot = [relay.at[way, p, 0], relay.at[way, p, pl.ds(1, 3)], relay.at[way, p, 4]]
+
+        def copy(src, dst):
+            return remote(src, dst, relay_send.at[way, p], relay_recv.at[way, p], rad=to)
+
+        first = [copy(a, b) for a, b in zip(edge, slot)]
+        return carries, carries & jnp.logical_not(last), copy(relay.at[way, p], relay.at[way, p]), first
 
     def seam(stage):
         for way in range(2):
@@ -126,19 +119,32 @@
             @pl.when(hops == stage)
             def _():
                 for p in range(half):
-                    carries, hands_on, copy, edge = seam_part(way, p)
+                    carries, hands_on, onward, first = seam_part(way, p)
                     if stage == 0:
                         @pl.when(carries)
                         def _():
-                            copy(edge).start()
+                            for a in first:
+                                a.start()
                     else:
                         @pl.when(carries)
                         def _():
-                            copy(relay.at[way, p]).wait_recv()
+                            onward.wait_recv()
 
                         @pl.when(hands_on)
                         def _():
-                            copy(relay.at[way, p]).start()
+                            onward.start()
+
+    seam(0)
+
+    @pl.when(has_out)
+    def _():
+        for c in outward:
+            c.start()
+
+    @pl.when(has_in)
+    def _():
+        for c in inward:
+            c.start()
 
     def seam_into_state():
         for way in range(2):
@@ -179,11 +185,11 @@
 
         for way in range(2):
             for p in range(half):
-                carries, hands_on, copy, edge = seam_part(way, p)
+                carries, hands_on, onward, first = seam_part(way, p)
 
                 @pl.when(hands_on)
                 def _():
-                    copy(relay.at[way, p]).wait_send()
+                    onward.wait_send()
 
     lane = lax.broadcasted_iota(jnp.int32, (SUB, LANES), 1)
     sub = lax.broadcasted_iota(jnp.int32, (SUB, LANES), 0)
@@ -218,7 +224,6 @@
         c.start()
     for c in loads[1]:
         c.wait()
-    seam(0)
     lax.fori_loop(1, tiles, packing, 0)
     for c in azimuthal[1]:
         c.start()
@@ -300,7 +305,7 @@
         lax.fori_loop(0, per, lambda p, _: (compute(row, c * per + p), 0)[1], 0)
 
     def turn_of(c):
-        return c * rows // early % rows
+        return (c % 2 * 4 + c // 2 % 2 * 2 + c // 4) * (rows // 8) % rows
 
     def first_leg(c, row):
         part = send.at[row, pl.ds(c * per, per)]
@@ -341,8 +346,8 @@
         if c == 0:
             for a in azimuthal[1]:
                 a.wait()
-        if c < half:
-            seam(c + 1)
+        if 1 <= c - early + half + 1 <= half:
+            seam(c - early + half + 1)
         if c == early - 1:
             radial_arrived()
             seam_into_state()
@@ -416,7 +421,7 @@
     rows, thetas, width = density.shape
     n = lax.axis_size("az")
     tiles = thetas // SUB
-    chunks, early = 8, 4
+    chunks, early = 8, 6
     per = tiles // chunks
     half = lax.axis_size("rad") // 2
     dma = pltpu.SemaphoreType.DMA

time: 135 us -> 132 us (0.978)
  Pallas kernels: 134 us -> 130 us
    pallas_call x1, Pallas kernels: 131 us -> 128 us  [per_device(): pl.pallas_call(functools.partial(kernel, chunks, early), out_shape=pltpu....]
where the time goes in v4:
time: 132 us; the launch traced here: 131 us
  Pallas kernels  130 us (98%)
    pallas_call x1, Pallas kernels, per_device(): pl.pallas_call(functools.partial(kernel, chunks, early), out_shape=pltpu....  128 us

profile of v4, /device:TPU:65, one launch (start us, length us, event | category | flops | bytes accessed | tf_op | source)
XLA Modules:
  0.0 131.1 jit_solution(9866986290300341357)
XLA Ops:
  0.6 128.0 %transport.1.landed = f32[16,5,64,256]{3,2,1,0:T(8,128)S(1)} custom-call(f32[16,64,256]{2,1,0:T(8,128)} %den.1, f32[3,16,64,256]{3,2,1,0:T(8,128)} %mom.1, f32[16,64,256]{2,1,0:T(8,128)} %en.1, s32[16]{0:T(128)} %shifts.1), custom_call_target="tpu_custom_call" | custom-call | tf_op jit(solution)/shard_map/transport/pallas_call | solution.py:430
  128.6 2.5 %deliver.1 = (f32[16,64,256]{2,1,0:T(8,128)}, f32[3,16,64,256]{3,2,1,0:T(8,128)}, f32[16,64,256]{2,1,0:T(8,128)}) custom-call(f32[16,5,64,256]{3,2,1,0:T(8,128)S(1)} %transport.1.landed), custom_call_target="tpu_custom_call" | custom-call | tf_op jit(solution)/shard_map/deliver/pallas_call | solution.py:464

commit v5 on v4

--- a/solution.py
+++ b/solution.py
@@ -24,9 +24,9 @@
 
 
 def peer(me, k):
-    y = (me // 4 + k // 4) % 4
-    x = (me // 2 + k // 2) % 2
-    core = (me + k) % 2
+    y = (me // 4 + k) % 4
+    x = (me // 2 + k // 4) % 2
+    core = (me + k // 8) % 2
     return y * 4 + x * 2 + core
 
 
@@ -80,116 +80,6 @@
     @pl.when(has_in)
     def _():
         pl.semaphore_signal(barrier, 1, device_id={"rad": pos - 1}, device_id_type=MESH)
-
-    pl.semaphore_wait(barrier, n + jnp.where(has_out, 1, 0) + jnp.where(has_in, 1, 0))
-
-    def radial(way, row, slot, to):
-        srcs = [den.at[row], mom.at[:, row], en.at[row]]
-        dsts = [st.at[0, slot], st.at[pl.ds(1, 3), slot], st.at[4, slot]]
-        return [remote(a, b, rad_send.at[way, j], rad_recv.at[way, j], rad=to) for j, (a, b) in enumerate(zip(srcs, dsts))]
-
-    outward = radial(0, rows - 1, 0, (pos + 1) % groups)
-    inward = radial(1, 0, rows + 1, (pos + groups - 1) % groups)
-
-    part_rows = tiles * SUB // half
-    low = pos < half
-    place = pos % half
-
-    def seam_part(way, p):
-        carries = jnp.where(low, p <= place, p >= place)
-        crossing = low if way == 0 else jnp.logical_not(low)
-        step = groups - 1 if way == 0 else 1
-        to = jnp.where(crossing & (p == place), across, (pos + step) % groups)
-        last = pos == (half if way == 0 else half - 1)
-        at = pl.ds(p * part_rows, part_rows)
-        row = rows - 1 if way == 0 else 0
-        edge = [den.at[row, at], mom.at[:, row, at], en.at[row, at]]
-        slot = [relay.at[way, p, 0], relay.at[way, p, pl.ds(1, 3)], relay.at[way, p, 4]]
-
-        def copy(src, dst):
-            return remote(src, dst, relay_send.at[way, p], relay_recv.at[way, p], rad=to)
-
-        first = [copy(a, b) for a, b in zip(edge, slot)]
-        return carries, carries & jnp.logical_not(last), copy(relay.at[way, p], relay.at[way, p]), first
-
-    def seam(stage):
-        for way in range(2):
-            hops = jnp.where(low, half - 1 - place, half - place) if way == 0 else jnp.where(low, place + 1, place)
-
-            @pl.when(hops == stage)
-            def _():
-                for p in range(half):
-                    carries, hands_on, onward, first = seam_part(way, p)
-                    if stage == 0:
-                        @pl.when(carries)
-                        def _():
-                            for a in first:
-                                a.start()
-                    else:
-                        @pl.when(carries)
-                        def _():
-                            onward.wait_recv()
-
-                        @pl.when(hands_on)
-                        def _():
-                            onward.start()
-
-    seam(0)
-
-    @pl.when(has_out)
-    def _():
-        for c in outward:
-            c.start()
-
-    @pl.when(has_in)
-    def _():
-        for c in inward:
-            c.start()
-
-    def seam_into_state():
-        for way in range(2):
-            @pl.when(pos == (half if way == 0 else half - 1))
-            def _():
-                for p in range(half):
-                    st[:, 0 if way == 0 else rows + 1, p * part_rows : (p + 1) * part_rows] = relay[way, p]
-
-    def radial_arrived():
-        @pl.when(has_in)
-        def _():
-            for c in outward:
-                c.wait_recv()
-
-        @pl.when(has_out)
-        def _():
-            for c in inward:
-                c.wait_recv()
-
-        @pl.when(at_inner)
-        def _():
-            st[:, 0] = st[:, 1]
-
-        @pl.when(at_outer)
-        def _():
-            st[:, rows + 1] = st[:, rows]
-
-    def radial_sent():
-        @pl.when(has_out)
-        def _():
-            for c in outward:
-                c.wait_send()
-
-        @pl.when(has_in)
-        def _():
-            for c in inward:
-                c.wait_send()
-
-        for way in range(2):
-            for p in range(half):
-                carries, hands_on, onward, first = seam_part(way, p)
-
-                @pl.when(hands_on)
-                def _():
-                    onward.wait_send()
 
     lane = lax.broadcasted_iota(jnp.int32, (SUB, LANES), 1)
     sub = lax.broadcasted_iota(jnp.int32, (SUB, LANES), 0)
@@ -220,8 +110,118 @@
     for c in loads[0]:
         c.wait()
     packing(0, 0)
+    pl.semaphore_wait(barrier, n + jnp.where(has_out, 1, 0) + jnp.where(has_in, 1, 0))
     for c in azimuthal[0]:
         c.start()
+
+    def radial(way, row, slot, to):
+        srcs = [den.at[row], mom.at[:, row], en.at[row]]
+        dsts = [st.at[0, slot], st.at[pl.ds(1, 3), slot], st.at[4, slot]]
+        return [remote(a, b, rad_send.at[way, j], rad_recv.at[way, j], rad=to) for j, (a, b) in enumerate(zip(srcs, dsts))]
+
+    outward = radial(0, rows - 1, 0, (pos + 1) % groups)
+    inward = radial(1, 0, rows + 1, (pos + groups - 1) % groups)
+
+    part_rows = tiles * SUB // half
+    low = pos < half
+    place = pos % half
+
+    def seam_part(way, p):
+        carries = jnp.where(low, p <= place, p >= place)
+        crossing = low if way == 0 else jnp.logical_not(low)
+        step = groups - 1 if way == 0 else 1
+        to = jnp.where(crossing & (p == place), across, (pos + step) % groups)
+        last = pos == (half if way == 0 else half - 1)
+        at = pl.ds(p * part_rows, part_rows)
+        row = rows - 1 if way == 0 else 0
+        edge = [den.at[row, at], mom.at[:, row, at], en.at[row, at]]
+        slot = [relay.at[way, p, 0], relay.at[way, p, pl.ds(1, 3)], relay.at[way, p, 4]]
+
+        def copy(src, dst):
+            return remote(src, dst, relay_send.at[way, p], relay_recv.at[way, p], rad=to)
+
+        first = [copy(a, b) for a, b in zip(edge, slot)]
+        return carries, carries & jnp.logical_not(last), copy(relay.at[way, p], relay.at[way, p]), first
+
+    def seam(stage):
+        for way in range(2):
+            hops = jnp.where(low, half - 1 - place, half - place) if way == 0 else jnp.where(low, place + 1, place)
+
+            @pl.when(hops == stage)
+            def _():
+                for p in range(half):
+                    carries, hands_on, onward, first = seam_part(way, p)
+                    if stage == 0:
+                        @pl.when(carries)
+                        def _():
+                            for a in first:
+                                a.start()
+                    else:
+                        @pl.when(carries)
+                        def _():
+                            onward.wait_recv()
+
+                        @pl.when(hands_on)
+                        def _():
+                            onward.start()
+
+    seam(0)
+
+    @pl.when(has_out)
+    def _():
+        for c in outward:
+            c.start()
+
+    @pl.when(has_in)
+    def _():
+        for c in inward:
+            c.start()
+
+    def seam_into_state():
+        for way in range(2):
+            @pl.when(pos == (half if way == 0 else half - 1))
+            def _():
+                for p in range(half):
+                    st[:, 0 if way == 0 else rows + 1, p * part_rows : (p + 1) * part_rows] = relay[way, p]
+
+    def radial_arrived():
+        @pl.when(has_in)
+        def _():
+            for c in outward:
+                c.wait_recv()
+
+        @pl.when(has_out)
+        def _():
+            for c in inward:
+                c.wait_recv()
+
+        @pl.when(at_inner)
+        def _():
+            st[:, 0] = st[:, 1]
+
+        @pl.when(at_outer)
+        def _():
+            st[:, rows + 1] = st[:, rows]
+
+    def radial_sent():
+        @pl.when(has_out)
+        def _():
+            for c in outward:
+                c.wait_send()
+
+        @pl.when(has_in)
+        def _():
+            for c in inward:
+                c.wait_send()
+
+        for way in range(2):
+            for p in range(half):
+                carries, hands_on, onward, first = seam_part(way, p)
+
+                @pl.when(hands_on)
+                def _():
+                    onward.wait_send()
+
     for c in loads[1]:
         c.wait()
     lax.fori_loop(1, tiles, packing, 0)

time: 132 us -> 129 us (0.977)
    pallas_call x1, Pallas kernels: 128 us -> 126 us  [per_device(): pl.pallas_call(functools.partial(kernel, chunks, early), out_shape=pltpu....]
where the time goes in v5:
time: 129 us
  Pallas kernels  129 us (100%)
    pallas_call x1, Pallas kernels, per_device(): pl.pallas_call(functools.partial(kernel, chunks, early), out_shape=pltpu....  126 us

profile of v5, /device:TPU:65, one launch (start us, length us, event | category | flops | bytes accessed | tf_op | source)
XLA Modules:
  0.0 129.3 jit_solution(17626349784368793106)
XLA Ops:
  0.6 126.1 %transport.1.landed = f32[16,5,64,256]{3,2,1,0:T(8,128)S(1)} custom-call(f32[16,64,256]{2,1,0:T(8,128)} %den.1, f32[3,16,64,256]{3,2,1,0:T(8,128)} %mom.1, f32[16,64,256]{2,1,0:T(8,128)} %en.1, s32[16]{0:T(128)} %shifts.1), custom_call_target="tpu_custom_call" | custom-call | tf_op jit(solution)/shard_map/transport/pallas_call | solution.py:430
  126.8 2.5 %deliver.1 = (f32[16,64,256]{2,1,0:T(8,128)}, f32[3,16,64,256]{3,2,1,0:T(8,128)}, f32[16,64,256]{2,1,0:T(8,128)}) custom-call(f32[16,5,64,256]{3,2,1,0:T(8,128)S(1)} %transport.1.landed), custom_call_target="tpu_custom_call" | custom-call | tf_op jit(solution)/shard_map/deliver/pallas_call | solution.py:464

commit v6 on v5

--- a/solution.py
+++ b/solution.py
@@ -52,7 +52,7 @@
             pltpu.make_async_copy(en.at[:, at], st.at[4, pl.ds(1, rows), at], in_sem.at[j, 2]),
         ]
 
-    loads = [load(0, 0, 2), load(1, 2, tiles - 2)]
+    loads = [load(0, 0, 1), load(1, 1, tiles - 1)]
     get_shifts = pltpu.make_async_copy(shifts, amounts, shift_sem)
     for part in loads:
         for c in part:
@@ -337,7 +337,7 @@
                 pl.when(jnp.logical_not(edge))(do)
             return 0
 
-        lax.fori_loop(0, rows, step, 0)
+        lax.fori_loop(1, n + 1, step, 0)
 
     for c in azimuthal[0]:
         c.wait()
@@ -390,7 +390,7 @@
 
             return 0
 
-        lax.fori_loop(0, n, give, 0)
+        lax.fori_loop(1, n + 1, give, 0)
 
     for c in range(chunks):
         wait_bytes(send.at[pl.ds(0, n - 1), pl.ds(c * per, per)], s1.at[c])
@@ -466,7 +466,7 @@
         out_shape=[jax.ShapeDtypeStruct(x.shape, f32) for x in (density, momenta, energy)],
         in_specs=[pl.BlockSpec(memory_space=pl.ANY)],
         out_specs=[pl.BlockSpec(memory_space=pl.ANY)] * 3,
-        scratch_shapes=[dma((4, FIELDS))],
+        scratch_shapes=[dma((1, FIELDS))],
         compiler_params=pltpu.CompilerParams(vmem_limit_bytes=2**20),
         name="deliver",
     )(landed)

time: 129 us -> 129 us (level)
  no operation moved by 1% of the time
where the time goes in v6:
time: 129 us
  Pallas kernels  128 us (99%)
    pallas_call x1, Pallas kernels, per_device(): pl.pallas_call(functools.partial(kernel, chunks, early), out_shape=pltpu....  126 us

profile of v6, /device:TPU:65, one launch (start us, length us, event | category | flops | bytes accessed | tf_op | source)
XLA Modules:
  0.0 129.1 jit_solution(6817260367693222842)
XLA Ops:
  0.6 126.0 %transport.1.landed = f32[16,5,64,256]{3,2,1,0:T(8,128)S(1)} custom-call(f32[16,64,256]{2,1,0:T(8,128)} %den.1, f32[3,16,64,256]{3,2,1,0:T(8,128)} %mom.1, f32[16,64,256]{2,1,0:T(8,128)} %en.1, s32[16]{0:T(128)} %shifts.1), custom_call_target="tpu_custom_call" | custom-call | tf_op jit(solution)/shard_map/transport/pallas_call | solution.py:430
  126.7 2.4 %deliver.1 = (f32[16,64,256]{2,1,0:T(8,128)}, f32[3,16,64,256]{3,2,1,0:T(8,128)}, f32[16,64,256]{2,1,0:T(8,128)}) custom-call(f32[16,5,64,256]{3,2,1,0:T(8,128)S(1)} %transport.1.landed), custom_call_target="tpu_custom_call" | custom-call | tf_op jit(solution)/shard_map/deliver/pallas_call | solution.py:464

commit v7 on v6

--- a/solution.py
+++ b/solution.py
@@ -24,7 +24,7 @@
 
 
 def peer(me, k):
-    y = (me // 4 + k) % 4
+    y = (me // 4 + k * (1 + me % 2 * 2)) % 4
     x = (me // 2 + k // 4) % 2
     core = (me + k // 8) % 2
     return y * 4 + x * 2 + core

time: 129 us -> 130 us (level); the launches traced: 129 us -> 129 us
  no operation moved by 1% of the time
where the time goes in v7:
time: 130 us; the launch traced here: 129 us
  Pallas kernels  128 us (98%)
    pallas_call x1, Pallas kernels, per_device(): pl.pallas_call(functools.partial(kernel, chunks, early), out_shape=pltpu....  126 us

profile of v7, /device:TPU:65, one launch (start us, length us, event | category | flops | bytes accessed | tf_op | source)
XLA Modules:
  0.0 128.7 jit_solution(17424618343116394079)
XLA Ops:
  0.6 125.6 %transport.1.landed = f32[16,5,64,256]{3,2,1,0:T(8,128)S(1)} custom-call(f32[16,64,256]{2,1,0:T(8,128)} %den.1, f32[3,16,64,256]{3,2,1,0:T(8,128)} %mom.1, f32[16,64,256]{2,1,0:T(8,128)} %en.1, s32[16]{0:T(128)} %shifts.1), custom_call_target="tpu_custom_call" | custom-call | tf_op jit(solution)/shard_map/transport/pallas_call | solution.py:430
  126.3 2.4 %deliver.1 = (f32[16,64,256]{2,1,0:T(8,128)}, f32[3,16,64,256]{3,2,1,0:T(8,128)}, f32[16,64,256]{2,1,0:T(8,128)}) custom-call(f32[16,5,64,256]{3,2,1,0:T(8,128)S(1)} %transport.1.landed), custom_call_target="tpu_custom_call" | custom-call | tf_op jit(solution)/shard_map/deliver/pallas_call | solution.py:464

commit v8 on v5

--- a/solution.py
+++ b/solution.py
@@ -167,15 +167,16 @@
 
     seam(0)
 
-    @pl.when(has_out)
-    def _():
-        for c in outward:
-            c.start()
-
-    @pl.when(has_in)
-    def _():
-        for c in inward:
-            c.start()
+    def radial_start():
+        @pl.when(has_out)
+        def _():
+            for c in outward:
+                c.start()
+
+        @pl.when(has_in)
+        def _():
+            for c in inward:
+                c.start()
 
     def seam_into_state():
         for way in range(2):
@@ -344,6 +345,7 @@
     for c in range(chunks):
         produce(c, "inside" if c < early else "every")
         if c == 0:
+            radial_start()
             for a in azimuthal[1]:
                 a.wait()
         if 1 <= c - early + half + 1 <= half:

time: 129 us -> 130 us (level)
  no operation moved by 1% of the time
where the time goes in v8:
time: 130 us; the launch traced here: 129 us
  Pallas kernels  128 us (98%)
    pallas_call x1, Pallas kernels, per_device(): pl.pallas_call(functools.partial(kernel, chunks, early), out_shape=pltpu....  126 us

profile of v8, /device:TPU:65, one launch (start us, length us, event | category | flops | bytes accessed | tf_op | source)
XLA Modules:
  0.0 129.0 jit_solution(9992296428980244337)
XLA Ops:
  0.6 125.9 %transport.1.landed = f32[16,5,64,256]{3,2,1,0:T(8,128)S(1)} custom-call(f32[16,64,256]{2,1,0:T(8,128)} %den.1, f32[3,16,64,256]{3,2,1,0:T(8,128)} %mom.1, f32[16,64,256]{2,1,0:T(8,128)} %en.1, s32[16]{0:T(128)} %shifts.1), custom_call_target="tpu_custom_call" | custom-call | tf_op jit(solution)/shard_map/transport/pallas_call | solution.py:432
  126.5 2.5 %deliver.1 = (f32[16,64,256]{2,1,0:T(8,128)}, f32[3,16,64,256]{3,2,1,0:T(8,128)}, f32[16,64,256]{2,1,0:T(8,128)}) custom-call(f32[16,5,64,256]{3,2,1,0:T(8,128)S(1)} %transport.1.landed), custom_call_target="tpu_custom_call" | custom-call | tf_op jit(solution)/shard_map/deliver/pallas_call | solution.py:466
